TPU v7x, 256 devices: a whole 4x4x8 slice. The times are simulated.
256 devices in a mesh: dp: 2 (over core), ctx: 32 (over z, y), head: 4 (over x).
Axes of the slice: x: 4, y: 4, z: 8, core: 2. Of those that a mesh axis runs over, the one named last changes fastest.
Arguments:
- query: bfloat16 [16384, 1024], P(('dp', 'ctx'), 'head'), parts along dimension 0, may hold values from -400 to 400
- key: bfloat16 [16384, 1024], P(('dp', 'ctx'), 'head'), parts along dimension 0, may hold values from -400 to 400
- value: bfloat16 [16384, 2048], P(('dp', 'ctx'), 'head'), parts along dimension 0, may hold values from -6 to 6
- out_grad: bfloat16 [16384, 2048], P(('dp', 'ctx'), 'head'), parts along dimension 0, may hold values from -6 to 6
- log_decay: float32 [16, 16384], P('head', ('dp', 'ctx')), parts along dimension 1, may hold values from -2 to 0
- beta: float32 [16, 16384], P('head', ('dp', 'ctx')), parts along dimension 1, may hold values from 0.05 to 0.95
- w_query: bfloat16 [2048, 1024], P(None, 'head'), may hold values from -0.125 to 0.125
- w_key: bfloat16 [2048, 1024], P(None, 'head'), may hold values from -0.125 to 0.125
- w_value: bfloat16 [2048, 2048], P(None, 'head'), may hold values from -0.125 to 0.125
Outputs:
- input_grad: bfloat16 [16384, 2048], P(('dp', 'ctx', 'head')), parts along dimension 0
- decay_grad: float32 [16, 16384], P('head', ('dp', 'ctx')), parts along dimension 1
- beta_grad: float32 [16, 16384], P('head', ('dp', 'ctx')), parts along dimension 1
There are 2 independent parts, one for each index of `dp`. A program takes and returns all parts, laid end to end along the dimension named above; an argument that names none is the same for every part. Nothing has to cross between parts.
All inputs are finite; a program needn't handle non-finite values.
Results may differ from a plain program's by a relative error of at most 0.0049.
Values sent between devices are 32-bit elements; how exact they have to be, the bound alone decides.
A program may use at most 128 MiB of HBM per device.

v0:
```python
from functools import partial

import jax
import jax.numpy as jnp
from jax import lax
from jax.sharding import PartitionSpec as P

STRETCH = 64


accurate_arithmetic_mode = lax.Precision.HIGHEST


def from_behind(value, axis, by):
    count = lax.axis_size(axis)
    pairs = [(i, i + by) for i in range(count) if 0 <= i + by < count]
    return lax.ppermute(value, axis, pairs)


def unit_rows(values):
    return values * lax.rsqrt(jnp.sum(values * values, axis=-1, keepdims=True) + 1e-06)


def by_block(matrix, count, width):
    blocks = matrix.shape[0] // STRETCH
    return matrix.reshape(blocks, STRETCH, count, width).transpose(0, 2, 1, 3)


def permute_order(query, key, value, log_decay, beta):
    heads_value, tok_rows = log_decay.shape
    width = value.shape[1] // heads_value
    heads_key = query.shape[1] // width
    blocks = tok_rows // STRETCH
    repeat = heads_value // heads_key
    query_normalized = jnp.repeat(
        unit_rows(by_block(query, heads_key, width)) * width ** (-0.5), repeat, axis=1
    )
    key_normalized = jnp.repeat(unit_rows(by_block(key, heads_key, width)), repeat, axis=1)
    value_rows = by_block(value, heads_value, width)
    gates = log_decay.reshape(heads_value, blocks, STRETCH).transpose(1, 0, 2)
    betas = beta.reshape(heads_value, blocks, STRETCH).transpose(1, 0, 2)
    return (query_normalized, key_normalized, value_rows, gates, betas)


def stretch_pieces(query_normalized, key_normalized, value_rows, gates, betas):
    length = gates.shape[0]
    cumulative = jnp.cumsum(gates)
    order_row = jnp.arange(length)[:, None]
    order_col = jnp.arange(length)[None, :]
    below_eq = order_row >= order_col
    below = order_row > order_col
    gaps = jnp.where(below_eq, cumulative[:, None] - cumulative[None, :], 0.0)
    within = jnp.where(below_eq, jnp.exp(gaps), 0.0)
    gains = jnp.exp(cumulative)
    key_dots = jnp.dot(key_normalized, key_normalized.T, precision=accurate_arithmetic_mode)
    system = jnp.eye(length, dtype=gates.dtype) + jnp.where(
        below, within * key_dots * betas[:, None], 0.0
    )
    empty_values = jax.scipy.linalg.solve_triangular(
        system, betas[:, None] * value_rows, lower=True
    )
    weights = jax.scipy.linalg.solve_triangular(
        system, (betas * gains)[:, None] * key_normalized, lower=True
    )
    toward_finish = jnp.exp(cumulative[-1] - cumulative)[:, None] * key_normalized
    mixing = within * jnp.dot(
        query_normalized, key_normalized.T, precision=accurate_arithmetic_mode
    )
    return (gains, toward_finish, empty_values, weights, mixing)


def stretch_run(memory_state, pieces, query_normalized):
    gains, toward_finish, empty_values, weights, mixing = pieces
    fresh = empty_values - jnp.dot(weights, memory_state, precision=accurate_arithmetic_mode)
    output = jnp.dot(
        gains[:, None] * query_normalized, memory_state, precision=accurate_arithmetic_mode
    ) + jnp.dot(mixing, fresh, precision=accurate_arithmetic_mode)
    state_next = gains[-1] * memory_state + jnp.dot(
        toward_finish.T, fresh, precision=accurate_arithmetic_mode
    )
    return (output, state_next)


def local_forward(state_in, query, key, value, log_decay, beta):
    parts = permute_order(query, key, value, log_decay, beta)

    def local_advance(memory_state, stretch_parts):
        query_normalized, key_normalized, value_rows, gates, betas = stretch_parts
        pieces = jax.vmap(stretch_pieces)(
            query_normalized, key_normalized, value_rows, gates, betas
        )
        output, state_next = jax.vmap(stretch_run)(memory_state, pieces, query_normalized)
        return (state_next, output)

    state_out, outputs = lax.scan(local_advance, state_in, parts)
    blocks, heads, length, width = outputs.shape
    return (outputs.transpose(0, 2, 1, 3).reshape(blocks * length, heads * width), state_out)


def composite(parts, grad_blocks):
    heads = parts[0].shape[1]
    width = parts[0].shape[3]
    identity_maps = jnp.broadcast_to(jnp.eye(width, dtype=jnp.float32), (heads, width, width))
    zero_maps = jnp.zeros((heads, width, width), jnp.float32)

    def composite_advance(carry, stretch_parts):
        overall_transition, overall_state, adjoint_state = carry
        query_normalized, key_normalized, value_rows, gates, betas, derivative_entries = (
            stretch_parts
        )
        gains, toward_finish, empty_values, weights, mixing = jax.vmap(stretch_pieces)(
            query_normalized, key_normalized, value_rows, gates, betas
        )
        single_transition = gains[:, -1, None, None] * identity_maps - jnp.einsum(
            "hck,hcj->hkj", toward_finish, weights, precision=accurate_arithmetic_mode
        )
        recurrent_matrix_lookups = gains[:, :, None] * query_normalized - jnp.einsum(
            "hts,hsk->htk", mixing, weights, precision=accurate_arithmetic_mode
        )
        adjoint_pulled = jnp.einsum(
            "iyh,iyx->ihx",
            recurrent_matrix_lookups,
            derivative_entries,
            precision=accurate_arithmetic_mode,
        )
        adjoint_state = adjoint_state + jnp.einsum(
            "gqm,gqu->gmu", overall_transition, adjoint_pulled, precision=accurate_arithmetic_mode
        )
        overall_state = jnp.einsum(
            "efs,esz->efz", single_transition, overall_state, precision=accurate_arithmetic_mode
        ) + jnp.einsum(
            "zfn,zfj->znj", toward_finish, empty_values, precision=accurate_arithmetic_mode
        )
        overall_transition = jnp.einsum(
            "hkj,hji->hki",
            single_transition,
            overall_transition,
            precision=accurate_arithmetic_mode,
        )
        return ((overall_transition, overall_state, adjoint_state), None)

    results, unused = lax.scan(
        composite_advance, (identity_maps, zero_maps, zero_maps), parts + (grad_blocks,)
    )
    return results


def apply_map(transition_maps, memory_states):
    return jnp.einsum(
        "efs,esz->efz", transition_maps, memory_states, precision=accurate_arithmetic_mode
    )


def per_device(query, key, value, out_grad, log_decay, beta, w_query, w_key, w_value):
    heads_value, tok_rows = log_decay.shape
    width = value.shape[1] // heads_value
    probe_matrix_whole = query.astype(jnp.float32)
    key_full = key.astype(jnp.float32)
    value_full = value.astype(jnp.float32)
    grad_full = out_grad.astype(jnp.float32)
    parts = permute_order(probe_matrix_whole, key_full, value_full, log_decay, beta)
    grad_blocks = by_block(grad_full, heads_value, width)
    overall_transition, overall_state, adjoint_state = composite(parts, grad_blocks)
    zero_states = jnp.zeros_like(overall_state)
    transposed = jnp.swapaxes(overall_transition, 1, 2)
    turns = lax.axis_size("ctx") - 1

    def forward_turn(turn, incoming):
        return from_behind(apply_map(overall_transition, incoming) + overall_state, "ctx", 1)

    def backward_turn(turn, incoming):
        return from_behind(apply_map(transposed, incoming) + adjoint_state, "ctx", -1)

    state_in = lax.fori_loop(0, turns, forward_turn, zero_states)
    costate_in = lax.fori_loop(0, turns, backward_turn, zero_states)
    outputs, pull = jax.vjp(
        partial(local_forward, state_in), probe_matrix_whole, key_full, value_full, log_decay, beta
    )
    grad_query, derivative_lookup_vector, grad_value, decay_grad, beta_grad = pull(
        (grad_full, costate_in)
    )
    grad_parts = (
        grad_query.astype(jnp.bfloat16),
        derivative_lookup_vector.astype(jnp.bfloat16),
        grad_value.astype(jnp.bfloat16),
    )
    matrices = (w_query, w_key, w_value)
    total = jnp.zeros(
        (tok_rows // lax.axis_size("head") * lax.axis_size("head"), w_query.shape[0]), jnp.float32
    )
    for grad_part, matrix in zip(grad_parts, matrices):
        total = total + jnp.einsum(
            "tc,dc->td", grad_part, matrix, preferred_element_type=jnp.float32
        )
    input_grad = lax.psum_scatter(total, "head", scatter_dimension=0, tiled=True).astype(
        jnp.bfloat16
    )
    return (input_grad, decay_grad, beta_grad)


def solution(mesh):
    in_specs = (
        P(("dp", "ctx"), "head"),
        P(("dp", "ctx"), "head"),
        P(("dp", "ctx"), "head"),
        P(("dp", "ctx"), "head"),
        P("head", ("dp", "ctx")),
        P("head", ("dp", "ctx")),
        P(None, "head"),
        P(None, "head"),
        P(None, "head"),
    )
    out_specs = (P(("dp", "ctx", "head"), None), P("head", ("dp", "ctx")), P("head", ("dp", "ctx")))
    return jax.shard_map(
        per_device, mesh=mesh, in_specs=in_specs, out_specs=out_specs, check_vma=False
    )
```

profile of v0, /device:TPU:64, one launch (start us, length us, event | category | flops | bytes accessed | tf_op | source)
XLA Modules:
  0.0 1445.5 jit_solution(12060235624285415581)
XLA Ops:
  21.4 138.8 %while.127 = (s32[]{:T(128)}, f32[4,128,128]{2,1,0:T(8,128)S(1)}, f32[4,128,128]{2,1,0:T(8,128)S(1)}, f32[4,128,128]{1,2,0:T(8,128)}, f32[4,4,64]{2,1,0:T(4,128)...) while((s32[]{:T(128)}, f32[4,128,128]{2,1,0:T(8,128)S(1)}, ...), condition=%wide.region_4.6_spmd.clone, body=%wide.region_2.5_spmd.clone.sunk | while | flops 579633408 | bytes 9320416 | solution.py:142
  24.9 20.4 %custom-call.40 = f32[4,1,64,64]{2,3,1,0:T(8,128)S(1)} custom-call(f32[4,1,64,64]{3,2,1,0:T(8,128)} %fusion.392), custom_call_target="InvertDiagBlocksLowerTriangular" | custom-call | tf_op jit(solution)/shard_map/while/body/eval_jaxpr/vmap(jit(_solve_triangular))/triangular_solve/custom-call.1 | solution.py:62
  59.5 20.4 %custom-call.40 = f32[4,1,64,64]{2,3,1,0:T(8,128)S(1)} custom-call(f32[4,1,64,64]{3,2,1,0:T(8,128)} %fusion.392), custom_call_target="InvertDiagBlocksLowerTriangular" | custom-call | tf_op jit(solution)/shard_map/while/body/eval_jaxpr/vmap(jit(_solve_triangular))/triangular_solve/custom-call.1 | solution.py:62
  94.3 20.4 %custom-call.40 = f32[4,1,64,64]{2,3,1,0:T(8,128)S(1)} custom-call(f32[4,1,64,64]{3,2,1,0:T(8,128)} %fusion.392), custom_call_target="InvertDiagBlocksLowerTriangular" | custom-call | tf_op jit(solution)/shard_map/while/body/eval_jaxpr/vmap(jit(_solve_triangular))/triangular_solve/custom-call.1 | solution.py:62
  129.0 20.4 %custom-call.40 = f32[4,1,64,64]{2,3,1,0:T(8,128)S(1)} custom-call(f32[4,1,64,64]{3,2,1,0:T(8,128)} %fusion.392), custom_call_target="InvertDiagBlocksLowerTriangular" | custom-call | tf_op jit(solution)/shard_map/while/body/eval_jaxpr/vmap(jit(_solve_triangular))/triangular_solve/custom-call.1 | solution.py:62
  160.3 384.9 %while.124 = (s32[]{:T(128)}, f32[4,128,128]{2,1,0:T(8,128)S(1)}, f32[4,128,128]{2,1,0:T(8,128)S(1)}, f32[4,128,128]{2,1,0:T(8,128)S(1)}, s32[]{:T(128)}) while((s32[]{:T(128)}, f32[4,128,128]{2,1,0:T(8,128)S(1)}, f32[4,128,128]{2,1,0:T(8,128)S(1)}, f32[4,128,128]{2,1,0:T(8,128)S(1)}, s32[]{:T(128)}) %tuple.226), condition=%wide.region_8.10_spmd, body=%wide.region_7.9_spmd.sunk | while | flops 100728832 | bytes 2097253 | solution.py:174
  548.8 142.3 %while.125 = (s32[]{:T(128)}, f32[4,128,128]{2,1,0:T(8,128)S(1)}, f32[4,4,64,64]{3,2,1,0:T(8,128)}, f32[4,4,64]{2,1,0:T(4,128)S(1)}, f32[4,4,128,64]{2,3,1,0:T(8...) while((s32[]{:T(128)}, f32[4,128,128]{2,1,0:T(8,128)S(1)}, ...), condition=%wide.region_11.13_spmd.clone.clone, body=%wide.region_9.12_spmd.clone.clone.sunk | while | flops 201995264 | bytes 5536157 | solution.py:95
  553.9 20.4 %custom-call.38 = f32[4,1,64,64]{2,3,1,0:T(8,128)S(1)} custom-call(f32[4,1,64,64]{3,2,1,0:T(8,128)} %select_bitcast_fusion.2), custom_call_target="InvertDiagBlocksLowerTriangular" | custom-call | tf_op jit(solution)/shard_map/jvp()/while/body/eval_jaxpr/vmap(jit(_solve_triangular))/triangular_solve/custom-call.1 | solution.py:59
  589.4 20.4 %custom-call.38 = f32[4,1,64,64]{2,3,1,0:T(8,128)S(1)} custom-call(f32[4,1,64,64]{3,2,1,0:T(8,128)} %select_bitcast_fusion.2), custom_call_target="InvertDiagBlocksLowerTriangular" | custom-call | tf_op jit(solution)/shard_map/jvp()/while/body/eval_jaxpr/vmap(jit(_solve_triangular))/triangular_solve/custom-call.1 | solution.py:59
  625.0 20.4 %custom-call.38 = f32[4,1,64,64]{2,3,1,0:T(8,128)S(1)} custom-call(f32[4,1,64,64]{3,2,1,0:T(8,128)} %select_bitcast_fusion.2), custom_call_target="InvertDiagBlocksLowerTriangular" | custom-call | tf_op jit(solution)/shard_map/jvp()/while/body/eval_jaxpr/vmap(jit(_solve_triangular))/triangular_solve/custom-call.1 | solution.py:59
  660.6 20.4 %custom-call.38 = f32[4,1,64,64]{2,3,1,0:T(8,128)S(1)} custom-call(f32[4,1,64,64]{3,2,1,0:T(8,128)} %select_bitcast_fusion.2), custom_call_target="InvertDiagBlocksLowerTriangular" | custom-call | tf_op jit(solution)/shard_map/jvp()/while/body/eval_jaxpr/vmap(jit(_solve_triangular))/triangular_solve/custom-call.1 | solution.py:59
  692.3 425.8 %while.123 = (s32[]{:T(128)}, f32[4,128,128]{2,1,0:T(8,128)S(1)}, f32[4,128,128]{2,1,0:T(8,128)S(1)}, f32[4,128,128]{2,1,0:T(8,128)S(1)}, s32[]{:T(128)}) while((s32[]{:T(128)}, f32[4,128,128]{2,1,0:T(8,128)S(1)}, f32[4,128,128]{2,1,0:T(8,128)S(1)}, f32[4,128,128]{2,1,0:T(8,128)S(1)}, s32[]{:T(128)}) %tuple.223), condition=%wide.region_6.8_spmd, body=%wide.region_5.7_spmd.sunk | while | flops 100728832 | bytes 2097253 | solution.py:175
  736.1 12.9 collective-permute-done
  752.1 13.5 collective-permute-done
  768.6 13.2 collective-permute-done
  889.7 13.1 collective-permute-done
  1023.7 12.7 collective-permute-done
  1039.3 13.0 collective-permute-done
  1121.1 249.1 %while.126 = (s32[]{:T(128)}, f32[4,128,128]{2,1,0:T(8,128)S(1)}, f32[4,4,64,128]{3,2,1,0:T(8,128)}, f32[4,4,64,128]{3,2,1,0:T(8,128)}, bf16[4,4,64,128]{3,2,1,0...) while((s32[]{:T(128)}, f32[4,128,128]{2,1,0:T(8,128)S(1)}, ...), condition=%wide.region_23.26_spmd.clone.clone, body=%wide.region_12.25_spmd.clone.clone.sunk | while | flops 580212736 | bytes 12549445 | solution.py:95
  1125.9 19.7 %custom-call.39 = f32[4,1,64,64]{2,3,1,0:T(8,128)S(1)} custom-call(f32[4,1,64,64]{3,2,1,0:T(8,128)S(1)} %fusion.358), custom_call_target="InvertDiagBlocksLowerTriangular" | custom-call | tf_op jit(solution)/shard_map/transpose(jvp())/while/body/eval_jaxpr/vmap(jit(_solve_triangular))/triangular_solve | solution.py:62
  1188.1 19.7 %custom-call.39 = f32[4,1,64,64]{2,3,1,0:T(8,128)S(1)} custom-call(f32[4,1,64,64]{3,2,1,0:T(8,128)S(1)} %fusion.358), custom_call_target="InvertDiagBlocksLowerTriangular" | custom-call | tf_op jit(solution)/shard_map/transpose(jvp())/while/body/eval_jaxpr/vmap(jit(_solve_triangular))/triangular_solve | solution.py:62
  1250.4 19.7 %custom-call.39 = f32[4,1,64,64]{2,3,1,0:T(8,128)S(1)} custom-call(f32[4,1,64,64]{3,2,1,0:T(8,128)S(1)} %fusion.358), custom_call_target="InvertDiagBlocksLowerTriangular" | custom-call | tf_op jit(solution)/shard_map/transpose(jvp())/while/body/eval_jaxpr/vmap(jit(_solve_triangular))/triangular_solve | solution.py:62
  1312.7 19.7 %custom-call.39 = f32[4,1,64,64]{2,3,1,0:T(8,128)S(1)} custom-call(f32[4,1,64,64]{3,2,1,0:T(8,128)S(1)} %fusion.358), custom_call_target="InvertDiagBlocksLowerTriangular" | custom-call | tf_op jit(solution)/shard_map/transpose(jvp())/while/body/eval_jaxpr/vmap(jit(_solve_triangular))/triangular_solve | solution.py:62
  1381.0 55.9 %reduce-scatter.2.cloned.1.call-done = f32[64,2048]{1,0:T(8,128)} async-done(((f32[256,2048]{1,0:T(8,128)}), f32[64,2048]{1,0:T(8,128)}) %reduce-scatter.2.cloned.1.call-update) | async-done | bytes 524304 | tf_op jit(solution)/shard_map/reduce_scatter | solution.py:195
  (708 shorter events, 1052.4 us)
Async XLA Ops:
  7.2 1429.7 %reduce-scatter.2.cloned.1.call-start = ((), (), s32[]{:S(2)}) async-start(), calls=%async_computation.1 | async-start | bytes 2621440 | tf_op jit(solution)/shard_map/reduce_scatter | solution.py:195
  161.4 12.2 collective-permute-start.1
  258.1 12.6 collective-permute-start.1
  271.9 13.0 collective-permute-start.1
  285.9 12.2 collective-permute-start.1
  382.6 12.7 collective-permute-start.1
  396.4 12.9 collective-permute-start.1
  719.9 13.2 collective-permute-start
  734.2 14.9 %collective-permute-start = (f32[4,128,128]{2,1,0:T(8,128)}, f32[4,128,128]{2,1,0:T(8,128)S(1)}, u32[]{:S(2)}, u32[]{:S(2)}) collective-permute-start(f32[4,128,128]{2,1,0:T(8,128)} %convolution_add_fusion.21), channel_id=1, source_target_pairs={{4,0},{8,4},{12,8},{16,12},{20,16},{24,20},{28,24},{32,28},{36,32}... | collective-permute-start | bytes 786440 | tf_op jit(solution)/shard_map/while/body/eval_jaxpr/ppermute | solution.py:17
  750.1 15.4 %collective-permute-start = (f32[4,128,128]{2,1,0:T(8,128)}, f32[4,128,128]{2,1,0:T(8,128)S(1)}, u32[]{:S(2)}, u32[]{:S(2)}) collective-permute-start(f32[4,128,128]{2,1,0:T(8,128)} %convolution_add_fusion.21), channel_id=1, source_target_pairs={{4,0},{8,4},{12,8},{16,12},{20,16},{24,20},{28,24},{32,28},{36,32}... | collective-permute-start | bytes 786440 | tf_op jit(solution)/shard_map/while/body/eval_jaxpr/ppermute | solution.py:17
  766.6 15.1 %collective-permute-start = (f32[4,128,128]{2,1,0:T(8,128)}, f32[4,128,128]{2,1,0:T(8,128)S(1)}, u32[]{:S(2)}, u32[]{:S(2)}) collective-permute-start(f32[4,128,128]{2,1,0:T(8,128)} %convolution_add_fusion.21), channel_id=1, source_target_pairs={{4,0},{8,4},{12,8},{16,12},{20,16},{24,20},{28,24},{32,28},{36,32}... | collective-permute-start | bytes 786440 | tf_op jit(solution)/shard_map/while/body/eval_jaxpr/ppermute | solution.py:17
  782.8 13.3 collective-permute-start
  858.1 13.0 collective-permute-start
  872.2 14.5 %collective-permute-start = (f32[4,128,128]{2,1,0:T(8,128)}, f32[4,128,128]{2,1,0:T(8,128)S(1)}, u32[]{:S(2)}, u32[]{:S(2)}) collective-permute-start(f32[4,128,128]{2,1,0:T(8,128)} %convolution_add_fusion.21), channel_id=1, source_target_pairs={{4,0},{8,4},{12,8},{16,12},{20,16},{24,20},{28,24},{32,28},{36,32}... | collective-permute-start | bytes 786440 | tf_op jit(solution)/shard_map/while/body/eval_jaxpr/ppermute | solution.py:17
  887.8 15.0 %collective-permute-start = (f32[4,128,128]{2,1,0:T(8,128)}, f32[4,128,128]{2,1,0:T(8,128)S(1)}, u32[]{:S(2)}, u32[]{:S(2)}) collective-permute-start(f32[4,128,128]{2,1,0:T(8,128)} %convolution_add_fusion.21), channel_id=1, source_target_pairs={{4,0},{8,4},{12,8},{16,12},{20,16},{24,20},{28,24},{32,28},{36,32}... | collective-permute-start | bytes 786440 | tf_op jit(solution)/shard_map/while/body/eval_jaxpr/ppermute | solution.py:17
  903.9 14.3 collective-permute-start
  919.2 13.0 collective-permute-start
  945.8 12.3 collective-permute-start
  1007.6 13.0 collective-permute-start
  1021.7 14.6 %collective-permute-start = (f32[4,128,128]{2,1,0:T(8,128)}, f32[4,128,128]{2,1,0:T(8,128)S(1)}, u32[]{:S(2)}, u32[]{:S(2)}) collective-permute-start(f32[4,128,128]{2,1,0:T(8,128)} %convolution_add_fusion.21), channel_id=1, source_target_pairs={{4,0},{8,4},{12,8},{16,12},{20,16},{24,20},{28,24},{32,28},{36,32}... | collective-permute-start | bytes 786440 | tf_op jit(solution)/shard_map/while/body/eval_jaxpr/ppermute | solution.py:17
  1037.4 14.9 %collective-permute-start = (f32[4,128,128]{2,1,0:T(8,128)}, f32[4,128,128]{2,1,0:T(8,128)S(1)}, u32[]{:S(2)}, u32[]{:S(2)}) collective-permute-start(f32[4,128,128]{2,1,0:T(8,128)} %convolution_add_fusion.21), channel_id=1, source_target_pairs={{4,0},{8,4},{12,8},{16,12},{20,16},{24,20},{28,24},{32,28},{36,32}... | collective-permute-start | bytes 786440 | tf_op jit(solution)/shard_map/while/body/eval_jaxpr/ppermute | solution.py:17
  1053.4 12.7 collective-permute-start
  1067.2 12.2 collective-permute-start
  1093.8 12.3 collective-permute-start
  (122 other events, 2684.0 us)
Sparse Core Ops, SparseCore 0:
  1379.1 57.7 reduce-scatter.1
where the time goes:
time: 1450 us
  waiting for transfers between devices  643 us (44%)
  other arithmetic  319 us (22%)
  matrix products  250 us (17%)
  starting transfers between devices  155 us (11%)
  local copies, waits for them, and re-layouts  62 us (4%)
  between operations  14.5 us (1%)
    ppermute x62, waiting for transfers between devices, from_behind(): return lax.ppermute(value, axis, pairs)  587 us
    another operation x20, other arithmetic, stretch_pieces(): jax.scipy.linalg.solve_triangular(system, (betas * gains)[:, None] * key_...  164 us
    ppermute x62, starting transfers between devices, from_behind(): return lax.ppermute(value, axis, pairs)  155 us
    another operation x12, other arithmetic, stretch_pieces(): jax.scipy.linalg.solve_triangular(system, betas[:, None] * value_rows, lo...  84.8 us
    dot_general x62, matrix products, apply_map(): jnp.einsum('efs,esz->efz', transition_maps, memory_states, precision=accu...  68 us
    reduce_scatter x1, waiting for transfers between devices, per_device(): lax.psum_scatter(total, 'head', scatter_dimension=0, tiled=True)  55.9 us
  transfers between devices with their start and end apart: 63, of which 63 were waited for; matrix products, arithmetic and copies ran while one was open for 0% of the time, Pallas kernels for 0%

commit v1 on v0

v1 whole, which is shorter than its diff:
```python
import functools

import jax
import jax.numpy as jnp
from jax import lax
from jax.experimental import pallas as pl
from jax.experimental.pallas import tpu as pltpu
from jax.sharding import PartitionSpec as P

MESH = pl.DeviceIdType.MESH
f32 = jnp.float32
bf16 = jnp.bfloat16
HD = 128
NY = 4
PAIR = 2
NN = (((1,), (0,)), ((), ()))
NT = (((1,), (1,)), ((), ()))
TN = (((0,), (0,)), ((), ()))


def split(x, n=2):
    if isinstance(x, (list, tuple)):
        return x
    if x.dtype == bf16:
        return [x]
    out = []
    for _ in range(n - 1):
        h = x.astype(bf16)
        out.append(h)
        x = x - h.astype(f32)
    out.append(x.astype(bf16))
    return out


def mm(a, b, dims=NN, n=2):
    a, b = split(a, n), split(b, n)
    total = None
    for i in reversed(range(len(a))):
        for j in reversed(range(len(b))):
            if i + j < n:
                term = lax.dot_general(a[i], b[j], dims, preferred_element_type=f32)
                total = term if total is None else total + term
    return total


def iotas(n):
    i = lax.broadcasted_iota(jnp.int32, (n, n), 0)
    j = lax.broadcasted_iota(jnp.int32, (n, n), 1)
    return i, j


def lower_inverses(blocks):
    n = HD
    i, j = iotas(n)
    eye = jnp.where(i == j, 1.0, 0.0).astype(f32)
    apart = i ^ j
    xs = [eye - jnp.where(apart == 1, b, 0.0) for b in blocks]
    level = 1
    while (1 << level) < n:
        here = (apart >> level) == 1
        xb = [x.astype(bf16) for x in xs]
        ys = [mm(jnp.where(here, b, 0.0).astype(bf16), x) for b, x in zip(blocks, xb)]
        xs = [x - mm(h, y.astype(bf16)) for x, h, y in zip(xs, xb, ys)]
        level += 1
    sp = [split(x) for x in xs]
    rs = [eye - x - mm(b, s) for b, x, s in zip(blocks, xs, sp)]
    return [x + mm(s, r) for x, s, r in zip(xs, sp, rs)]


def kernel(
    nx, groups,
    q_ref, k_ref, v_ref, do_ref, ld_ref, be_ref, wq_hbm, wk_hbm, wv_hbm,
    ig_ref, dld_ref, dbe_ref,
    wq, wk, wv,
    qs, ks, qn, kn, gam, th, tl, ub, wm, duo,
    snd1, rcv1, snd2, rcv2, st, snd3, rcv3,
    gbuf, pd2, pr, pl_, r2, rin,
    wsem, s1, v1, s2, v2, s3, v3, s4, v4,
):
    rows = q_ref.shape[0]
    heads = ld_ref.shape[0]
    kheads = q_ref.shape[1] // HD
    rep = heads // kheads
    ctx = lax.axis_index("ctx")
    me = lax.axis_index("head")
    z, y = ctx // NY, ctx % NY
    zg, kind = z // PAIR, z % PAIR
    cpg = PAIR * NY
    here = kind * NY + y
    pos = zg + kind * (groups - 1 - 2 * zg)
    up, down = (me + 1) % nx, (me + nx - 1) % nx

    def at(zz, yy):
        return {"ctx": zz * NY + yy}

    barrier = pltpu.get_barrier_semaphore()
    for d in range(1, cpg):
        c = (here + d) % cpg
        pl.semaphore_signal(barrier, inc=1, device_id=at(zg * PAIR + c // NY, c % NY), device_id_type=MESH)
    for d in range(1, groups):
        g = (zg + d) % groups
        pl.semaphore_signal(barrier, inc=1, device_id=at(g * PAIR + kind, y), device_id_type=MESH)
    for n in (up, down):
        pl.semaphore_signal(barrier, inc=1, device_id={"head": n}, device_id_type=MESH)

    loads = [
        pltpu.make_async_copy(a, b, wsem.at[i])
        for i, (a, b) in enumerate(((wq_hbm, wq), (wk_hbm, wk), (wv_hbm, wv)))
    ]
    for load in loads:
        load.start()

    i, j = iotas(rows)
    lower, strict = i >= j, i > j
    tri = jnp.where(lower, 1.0, 0.0).astype(bf16)
    unit = jnp.where(i == j, 1.0, 0.0).astype(bf16)
    ld = jnp.concatenate([ld_ref[...]] * 4, axis=0)
    be = jnp.concatenate([be_ref[...]] * 4, axis=0)
    lds = split(ld, 3)
    c_cols = mm(tri, lds, NT, 3)
    c_rows = mm(lds, tri, NT, 3)
    b_cols = mm(unit, split(be, 3), NT, 3)
    c_col = [c_cols[:, h : h + 1] for h in range(heads)]
    b_col = [b_cols[:, h : h + 1] for h in range(heads)]
    gamma = [jnp.exp(c) for c in c_col]
    c_end = [c[rows - 1 :, :] for c in c_col]
    gend = [jnp.exp(e - c) for e, c in zip(c_end, c_col)]

    i1, j1 = iotas(HD)
    eye = jnp.where(i1 == j1, 1.0, 0.0).astype(f32)

    scale = HD**-0.5
    kk, qk = [], []
    for g in range(kheads):
        cols = slice(g * HD, (g + 1) * HD)
        qf, kf = q_ref[:, cols].astype(f32), k_ref[:, cols].astype(f32)
        rq = lax.rsqrt(jnp.sum(qf * qf, axis=1, keepdims=True) + 1e-6)
        rk = lax.rsqrt(jnp.sum(kf * kf, axis=1, keepdims=True) + 1e-6)
        qu, ku = qf * rq, kf * rk
        qn[g], kn[g] = qu, ku
        qsp, ksp = split(qu * scale), split(ku)
        for t in range(2):
            qs[g, t], ks[g, t] = qsp[t], ksp[t]
        kk.append(mm(ksp, ksp, NT))
        qk.append(mm(qsp, ksp, NT))

    blocks, corners = [], []
    mix = []
    for h in range(heads):
        w = jnp.where(lower, jnp.exp(jnp.minimum(c_col[h] - c_rows[h : h + 1, :], 0.0)), 0.0)
        gam[h] = w
        low = jnp.where(strict, w * kk[h // rep], 0.0) * b_col[h]
        mix.append(split(w * qk[h // rep]))
        blocks += [low[:HD, :HD], low[HD:, HD:]]
        corners.append(low[HD:, :HD])
    inv = [split(x) for x in lower_inverses(blocks)]
    mids = [mm(corners[h], inv[2 * h]) for h in range(heads)]
    inv21 = [split(-mm(inv[2 * h + 1], mids[h])) for h in range(heads)]
    zero = jnp.zeros((HD, HD), bf16)
    for h in range(heads):
        for t, ref in enumerate((th, tl)):
            ref[h, :HD, :HD] = inv[2 * h][t]
            ref[h, :HD, HD:] = zero
            ref[h, HD:, :HD] = inv21[h][t]
            ref[h, HD:, HD:] = inv[2 * h + 1][t]

    def head(ref, h):
        return ref[:, h * HD : (h + 1) * HD]

    def send1(h, kk_):
        slot = here + kk_ * (cpg - 1 - 2 * here)
        return pltpu.make_async_remote_copy(
            src_ref=snd1.at[h, kk_], dst_ref=rcv1.at[slot],
            send_sem=s1.at[h, kk_], recv_sem=v1.at[slot],
            device_id=at(zg * PAIR + kk_, h), device_id_type=MESH,
        )

    def mine(h, kk_):
        return (y == h) & (kind == kk_)

    def dispatch(h, kk_):
        slot = here + kk_ * (cpg - 1 - 2 * here)

        @pl.when(mine(h, kk_))
        def _():
            rcv1[slot] = snd1[h, kk_]

        @pl.when(jnp.logical_not(mine(h, kk_)))
        def _():
            send1(h, kk_).start()

    for h in range(heads):
        g = h // rep
        ksp = (ks[g, 0], ks[g, 1])
        ku, qu = kn[g], qn[g]
        tsp = (th[h], tl[h])
        right = jnp.concatenate([b_col[h] * head(v_ref, h).astype(f32), (b_col[h] * gamma[h]) * ku], axis=1)
        uw = mm(tsp, right)
        ub[h], wm[h] = uw[:, :HD], uw[:, HD:]
        uws = split(uw)
        kend = split(gend[h] * ku)
        ba = mm(kend, uws, TN)
        a = jnp.exp(c_end[h]) * eye - ba[:, HD:]
        snd1[h, 0, 0] = a
        snd1[h, 0, 1] = ba[:, :HD]
        snd1[h, 1, 0] = a.T
        d = mm(mix[h], head(do_ref, h), TN)
        duo[h] = d
        wsp = [t[:, HD:] for t in uws]
        snd1[h, 1, 1] = mm((gamma[h] * scale) * qu, head(do_ref, h), TN) - mm(wsp, d, TN)

    pl.semaphore_wait(barrier, cpg + groups)
    for h in range(heads):
        for kk_ in range(PAIR):
            dispatch(h, kk_)

    def wait1(s):
        @pl.when(s != here + kind * (cpg - 1 - 2 * here))
        def _():
            pltpu.make_async_remote_copy(
                src_ref=snd1.at[0, 0], dst_ref=rcv1.at[s], send_sem=s1.at[0, 0], recv_sem=v1.at[s],
                device_id=at(z, y), device_id_type=MESH,
            ).wait_recv()

    for s in range(cpg):
        wait1(s)

    def after(second, first):
        (a2, b2), (a1, b1) = second, first
        r = mm(a2, jnp.concatenate([a1, b1], axis=1))
        return r[:, :HD], r[:, HD:] + b2

    maps = [(rcv1[s, 0], rcv1[s, 1]) for s in range(cpg)]
    two = [after(maps[2 * t + 1], maps[2 * t]) for t in range(cpg // 2)]
    four = [after(two[1], two[0]), after(two[3], two[2])]
    whole = after(four[1], four[0])
    snd2[0], snd2[1] = whole

    def send2(src, dst):
        gg = dst + kind * (groups - 1 - 2 * dst)
        lo = 1 if src == 0 else 0
        return pltpu.make_async_remote_copy(
            src_ref=snd2.at[lo:], dst_ref=rcv2.at[src, lo:],
            send_sem=s2.at[dst], recv_sem=v2.at[src],
            device_id=at(gg * PAIR + kind, y), device_id_type=MESH,
        )

    for src in range(groups - 1):
        @pl.when(pos == src)
        def _():
            for dst in reversed(range(src + 1, groups)):
                send2(src, dst).start()

    pre = [maps[0], two[0], after(maps[2], two[0]), four[0]]
    pre += [after(maps[4], four[0]), after(two[2], four[0])]
    pre.append(after(maps[6], pre[5]))

    st[...] = jnp.zeros_like(st)
    for dst in range(1, groups):
        @pl.when(pos == dst)
        def _():
            for src in range(dst):
                send2(src, dst).wait_recv()
            state = rcv2[0, 1]
            for src in range(1, dst):
                state = mm(rcv2[src, 0], state) + rcv2[src, 1]
            st[...] = state

    state = st[...]
    ssp = split(state)
    snd3[0] = state
    for s in range(1, cpg):
        a, b = pre[s - 1]
        snd3[s] = mm(a, ssp) + b

    def send3(d):
        c = (here + d) % cpg
        s = c + kind * (cpg - 1 - 2 * c)
        return pltpu.make_async_remote_copy(
            src_ref=snd3.at[s], dst_ref=rcv3.at[y, kind],
            send_sem=s3.at[d], recv_sem=v3.at[y, kind],
            device_id=at(zg * PAIR + c // NY, c % NY), device_id_type=MESH,
        )

    for d in range(1, cpg):
        send3(d).start()
    rcv3[y, kind] = snd3[here + kind * (cpg - 1 - 2 * here)]

    def wait3(h, kk_):
        @pl.when(jnp.logical_not(mine(h, kk_)))
        def _():
            pltpu.make_async_remote_copy(
                src_ref=snd3.at[0], dst_ref=rcv3.at[h, kk_], send_sem=s3.at[0], recv_sem=v3.at[h, kk_],
                device_id=at(z, y), device_id_type=MESH,
            ).wait_recv()

    for h in range(heads):
        for kk_ in range(PAIR):
            wait3(h, kk_)

    ones = jnp.ones((16, HD), bf16)
    for g in range(kheads):
        ku, qu = kn[g], qn[g]
        ksp, qsp = (ks[g, 0], ks[g, 1]), (qs[g, 0], qs[g, 1])
        qhat = qu * scale
        dq_sum = dk_sum = None
        for h in range(g * rep, (g + 1) * rep):
            s, c = rcv3[h, 0], rcv3[h, 1]
            ssp, csp = split(s), split(c)
            w, do = gam[h], head(do_ref, h)
            kend = gend[h] * ku
            u = ub[h] - mm(wm[h], ssp)
            usp = split(u)
            du = duo[h] + mm(kend, csp)
            dr = mm((th[h], tl[h]), du, TN)
            rsp = split(dr)
            dm = split(mm(do, usp, NT) * w)
            dl = split(jnp.where(strict, -(mm(rsp, usp, NT) * w), 0.0))
            dq = mm(dm, ksp) + gamma[h] * mm(do, ssp, NT)
            e = mm(dl, ksp) - gamma[h] * mm(rsp, ssp, NT)
            ug = gend[h] * mm(usp, csp, NT)
            dkw = mm(dm, qsp, TN) + mm(dl, b_col[h] * ku, TN) + ug
            left = b_col[h] * e
            dk = left + dkw
            gbuf[:, (2 * kheads + h) * HD : (2 * kheads + h + 1) * HD] = (b_col[h] * dr).astype(bf16)
            rate = mm(ones, dr * head(v_ref, h).astype(f32) + ku * e, NT, 3)
            dbe_ref[h : h + 1, :] = rate[:1, :]
            dcum = mm(ones, qhat * dq + ku * (left - dkw), NT, 3)
            ends = jnp.sum(ku * ug, axis=0, keepdims=True) + jnp.exp(c_end[h]) * jnp.sum(c * s, axis=0, keepdims=True)
            dld = mm(dcum, tri, NN, 3) + jnp.sum(ends, axis=1, keepdims=True)
            dld_ref[h : h + 1, :] = dld[:1, :]
            dq_sum = dq if dq_sum is None else dq_sum + dq
            dk_sum = dk if dk_sum is None else dk_sum + dk
        for x_ref, unit_rows, grad, at_col, mult in (
            (q_ref, qu, dq_sum, g, scale), (k_ref, ku, dk_sum, kheads + g, 1.0),
        ):
            xf = x_ref[:, g * HD : (g + 1) * HD].astype(f32)
            r = lax.rsqrt(jnp.sum(xf * xf, axis=1, keepdims=True) + 1e-6) * mult
            out = r * (grad - unit_rows * jnp.sum(unit_rows * grad, axis=1, keepdims=True))
            gbuf[:, at_col * HD : (at_col + 1) * HD] = out.astype(bf16)

    for load in loads:
        load.wait()
    part = rows // nx
    half = wq.shape[0] // 2
    kw = kheads * HD

    def project(dest, side):
        grads = gbuf[pl.ds(pl.multiple_of(dest * part, part), part), :]
        outs = slice(side * half, (side + 1) * half)
        total = lax.dot_general(grads[:, :kw], wq[outs, :], NT, preferred_element_type=f32)
        total += lax.dot_general(grads[:, kw : 2 * kw], wk[outs, :], NT, preferred_element_type=f32)
        total += lax.dot_general(grads[:, 2 * kw :], wv[outs, :], NT, preferred_element_type=f32)
        return total

    def hop(src, dst, n, to):
        return pltpu.make_async_remote_copy(
            src_ref=src, dst_ref=dst, send_sem=s4.at[n], recv_sem=v4.at[n],
            device_id={"head": to}, device_id_type=MESH,
        )

    hops = [
        hop(pd2.at[0], r2.at[0], 0, up), hop(pd2.at[1], r2.at[1], 1, down),
        hop(pr.at[1], rin.at[0, 1], 2, up), hop(pl_.at[0], rin.at[1, 0], 3, down),
        hop(pr.at[0], rin.at[0, 0], 4, up), hop(pl_.at[1], rin.at[1, 1], 5, down),
    ]
    far = (me + 2) % nx
    pd2[0] = project(far, 0)
    hops[0].start()
    pd2[1] = project(far, 1)
    hops[1].start()
    pr[1] = project(up, 1)
    hops[2].start()
    pl_[0] = project(down, 0)
    hops[3].start()
    pr[0] = project(up, 0)
    pl_[1] = project(down, 1)
    hops[0].wait_recv()
    pr[0] = pr[0] + r2[0]
    hops[4].start()
    hops[1].wait_recv()
    pl_[1] = pl_[1] + r2[1]
    hops[5].start()
    own = [project(me, 0), project(me, 1)]
    for n in (2, 3, 4, 5):
        hops[n].wait_recv()
    for side in range(2):
        total = own[side] + rin[0, side] + rin[1, side]
        ig_ref[:, side * half : (side + 1) * half] = total.astype(bf16)

    for n in range(6):
        hops[n].wait_send()
    for d in range(1, cpg):
        send3(d).wait_send()
    for src in range(groups - 1):
        @pl.when(pos == src)
        def _():
            for dst in range(src + 1, groups):
                send2(src, dst).wait_send()
    for h in range(heads):
        for kk_ in range(PAIR):
            @pl.when(jnp.logical_not(mine(h, kk_)))
            def _():
                send1(h, kk_).wait_send()


def solution(mesh):
    nx = mesh.shape["head"]
    groups = mesh.shape["ctx"] // (NY * PAIR)

    def per_device(q, k, v, do, ld, be, wq, wk, wv):
        rows, heads = q.shape[0], ld.shape[0]
        kheads = q.shape[1] // HD
        model = wq.shape[0]
        part, half = rows // nx, model // 2
        cpg = PAIR * NY
        vmem = pl.BlockSpec(memory_space=pltpu.VMEM)
        hbm = pl.BlockSpec(memory_space=pl.ANY)

        def buf(*shape, dtype=f32):
            return pltpu.VMEM(shape, dtype)

        dma = pltpu.SemaphoreType.DMA
        scratch = [
            buf(*wq.shape, dtype=bf16), buf(*wk.shape, dtype=bf16), buf(*wv.shape, dtype=bf16),
            buf(kheads, 2, rows, HD, dtype=bf16), buf(kheads, 2, rows, HD, dtype=bf16),
            buf(kheads, rows, HD), buf(kheads, rows, HD),
            buf(heads, rows, rows),
            buf(heads, rows, rows, dtype=bf16), buf(heads, rows, rows, dtype=bf16),
            buf(heads, rows, HD), buf(heads, rows, HD), buf(heads, rows, HD),
            buf(heads, PAIR, 2, HD, HD), buf(cpg, 2, HD, HD),
            buf(2, HD, HD), buf(groups - 1, 2, HD, HD), buf(HD, HD),
            buf(cpg, HD, HD), buf(heads, PAIR, HD, HD),
            buf(rows, (2 * kheads + heads) * HD, dtype=bf16),
            buf(2, part, half), buf(2, part, half), buf(2, part, half),
            buf(2, part, half), buf(2, 2, part, half),
            dma((3,)), dma((heads, PAIR)), dma((cpg,)), dma((groups,)), dma((groups,)),
            dma((cpg,)), dma((heads, PAIR)), dma((6,)), dma((6,)),
        ]
        return pl.pallas_call(
            functools.partial(kernel, nx, groups),
            out_shape=(
                jax.ShapeDtypeStruct((part, model), bf16),
                jax.ShapeDtypeStruct(ld.shape, f32),
                jax.ShapeDtypeStruct(be.shape, f32),
            ),
            in_specs=[vmem] * 6 + [hbm] * 3,
            out_specs=(vmem, vmem, vmem),
            scratch_shapes=scratch,
            compiler_params=pltpu.CompilerParams(
                collective_id=0, has_side_effects=True, vmem_limit_bytes=56 << 20
            ),
            name="delta_backward",
        )(q, k, v, do, ld, be, wq, wk, wv)

    row = P(("dp", "ctx"), "head")
    gate = P("head", ("dp", "ctx"))
    weight = P(None, "head")
    return jax.shard_map(
        per_device, mesh=mesh,
        in_specs=(row, row, row, row, gate, gate, weight, weight, weight),
        out_specs=(P(("dp", "ctx", "head"), None), gate, gate),
        check_vma=False,
    )
```

time: 1450 us -> 74.9 us (0.05)
  waiting for transfers between devices: 643 us -> 0 us
  other arithmetic: 319 us -> 0 us
  matrix products: 250 us -> 0 us
  starting transfers between devices: 155 us -> 0 us
  Pallas kernels: 0 us -> 69.5 us
  local copies, waits for them, and re-layouts: 62 us -> 4.22 us
    ppermute x62 -> x0, waiting for transfers between devices: 587 us -> none  [from_behind(): return lax.ppermute(value, axis, pairs)]
    another operation x62 -> x0, other arithmetic: 263 us -> none  [the longest x20 164 us: stretch_pieces(): jax.scipy.linalg.solve_triangular(system, (betas * gains)[:, None] * key_...]
    dot_general x173 -> x0, matrix products: 212 us -> none  [the longest x62 68 us: apply_map(): jnp.einsum('efs,esz->efz', transition_maps, memory_states, precision=accu...]
    ppermute x62 -> x0, starting transfers between devices: 155 us -> none  [from_behind(): return lax.ppermute(value, axis, pairs)]
    pallas_call x0 -> x1, Pallas kernels: none -> 69.5 us  [per_device(): pl.pallas_call(functools.partial(kernel, nx, groups), out_shape=(jax.Shap...]
    reduce_scatter x1 -> x0, waiting for transfers between devices: 55.9 us -> none  [per_device(): lax.psum_scatter(total, 'head', scatter_dimension=0, tiled=True)]
    another operation x32 -> x0, matrix products: 37.4 us -> none  [the longest x16 21.6 us: stretch_pieces(): jax.scipy.linalg.solve_triangular(system, betas[:, None] * value_rows, lo...]
    reduce_sum x22 -> x0, other arithmetic: 21.1 us -> none  [the longest x4 6.57 us: stretch_run(): gains[-1] * memory_state]
  transfers between devices with their start and end apart: 63 -> 0, of which waited for: 63 -> 0; matrix products, arithmetic and copies ran while one was open for 0% -> 0% of each run, Pallas kernels for 0% -> 0%
where the time goes in v1:
time: 74.9 us; the launch traced here: 74.4 us
  Pallas kernels  69.5 us (93%)
  local copies, waits for them, and re-layouts  4.22 us (6%)
    pallas_call x1, Pallas kernels, per_device(): pl.pallas_call(functools.partial(kernel, nx, groups), out_shape=(jax.Shap...  69.5 us
    unnamed x3, local copies, waits for them, and re-layouts  4.22 us

profile of v1, /device:TPU:64, one launch (start us, length us, event | category | flops | bytes accessed | tf_op | source)
XLA Modules:
  0.0 74.4 jit_solution(6878844123573472439)
XLA Ops:
  0.6 69.5 %delta_backward.1 = (bf16[64,2048]{1,0:T(8,128)(2,1)}, f32[4,256]{1,0:T(4,128)}, f32[4,256]{1,0:T(4,128)}) custom-call(bf16[256,256]{1,0:T(8,128)(2,1)} %q_ref.1, bf16[256,256]{1,0:T(8,128)(2,1)} %k_ref.1, bf16[256,512]{1,0:T(8,128)(2,1)} %v_ref.1, bf16[256,512]{1,0:T(8,128)(2,1)} %do_ref.1, f32[4,256]{1,0:T(4,128)} %ld_ref.1, f32[4,256]{1,0:T(4,128)} %be_ref.1, ...), custom_call_target="tpu_custom_call" | custom-call | tf_op jit(solution)/shard_map/delta_backward/pallas_call | solution.py:440
  70.2 1.7 %copy.15 = bf16[64,2048]{1,0:T(8,128)(2,1)} copy(bf16[64,2048]{1,0:T(8,128)(2,1)} %get-tuple-element.6) | data formatting | bytes 524288
  71.8 1.3 %copy.16 = f32[4,256]{1,0:T(4,128)} copy(f32[4,256]{1,0:T(4,128)} %get-tuple-element.7) | data formatting | bytes 8192
  73.1 1.3 %copy.17 = f32[4,256]{1,0:T(4,128)} copy(f32[4,256]{1,0:T(4,128)} %get-tuple-element.8) | data formatting | bytes 8192
